TPU v7x, 128 devices: a whole 4x4x4 slice. The times are simulated.
128 devices in a mesh: dp: 8 (over x, core), seq: 16 (over z, y).
Axes of the slice: x: 4, y: 4, z: 4, core: 2. Of those that a mesh axis runs over, the one named last changes fastest.
Arguments:
- trunk: bfloat16 [8, 4096, 1536], P('dp', 'seq'), may hold values from -34 to 34
- skip: bfloat16 [8, 8192, 1536], P('dp', 'seq'), may hold values from -6 to 6
- valid_bins: int32 [8], P('dp'), may hold values from 2048 to 4096, as said below
- query_weight: bfloat16 [1536, 256], replicated
- key_weight: bfloat16 [1536, 256], replicated
- value_weight: bfloat16 [1536, 768], replicated, may hold values from -0.15625 to 0.15625
- out_weight: bfloat16 [768, 1536], replicated, may hold values from -0.21875 to 0.21875
- depth_weight: float32 [3, 1536], replicated, may hold values from -3 to 3
- point_weight: bfloat16 [1536, 1536], replicated, may hold values from -0.15625 to 0.15625
- cotangent: bfloat16 [8, 8192, 1536], P('dp', 'seq'), may hold values from -6 to 6
Outputs:
- grad_pointwise: bfloat16 [1536, 1536], replicated
- grad_depthwise: float32 [3, 1536], replicated
- grad_skip: bfloat16 [8, 8192, 1536], P('dp', 'seq')
Inputs may be any that keep to these rules, and one draw needn't show every extreme that they name: Bins at or past a window's valid_bins are padding; in every draw some window is whole.
All inputs are finite; a program needn't handle non-finite values.
Results may differ from a plain program's by a relative error of at most 0.017.
Values may be sent and summed in bfloat16 or wider, within the bound.
No kernel may reach another device: no remote copies, remote signals or barrier semaphores. Data moves between devices by JAX's collectives and lax.ppermute only.
A program may use at most 128 MiB of HBM per device.

v0:
```python
from functools import partial
import math
import jax
import jax.numpy as jnp
from jax import lax
from jax.sharding import PartitionSpec as P

H = 4
DH = 64
DV = 192


def padded_2(cells, sides, width):
    for axis, dim in sides:
        count = lax.axis_size(axis)
        ends = count - 1
        head = lax.slice_in_dim(cells, 0, width, axis=dim)
        tail = lax.slice_in_dim(cells, cells.shape[dim] - width, cells.shape[dim], axis=dim)
        cells = jnp.concatenate(
            [
                lax.ppermute(tail, axis, [(i, (i + 1) % count) for i in range(ends)]),
                cells,
                lax.ppermute(head, axis, [((i + 1) % count, i) for i in range(ends)]),
            ],
            axis=dim,
        )
    return cells


def local(
    trunk,
    skip,
    valid_bins,
    query_weight,
    key_weight,
    value_weight,
    out_weight,
    depth_weight,
    point_weight,
    cotangent,
):
    tokens = trunk[0]
    row_count = tokens.shape[0]
    score_scale = 1.0 / math.sqrt(DH)
    queries = (
        jnp.dot(tokens, query_weight, preferred_element_type=jnp.float32)
        .astype(jnp.bfloat16)
        .reshape(row_count, H, DH)
    )
    keys = jnp.dot(tokens, key_weight, preferred_element_type=jnp.float32).astype(jnp.bfloat16)
    values = jnp.dot(tokens, value_weight, preferred_element_type=jnp.float32).astype(jnp.bfloat16)
    limit = valid_bins[0]
    running_max = jnp.full((H, row_count), -1e30, jnp.float32)
    weighted = jnp.zeros((row_count, H, DV), jnp.float32)
    key_piece = lax.all_gather(keys, "seq", axis=0, tiled=True)
    value_piece = lax.all_gather(values, "seq", axis=0, tiled=True)
    width = key_piece.shape[0]
    key_heads = key_piece.reshape(width, H, DH)
    value_heads = value_piece.reshape(width, H, DV)
    scores = (
        jnp.einsum("qhd,khd->hqk", queries, key_heads, preferred_element_type=jnp.float32)
        * score_scale
    )
    places = jnp.arange(width, dtype=jnp.int32)
    scores = jnp.where(places[None, None, :] < limit, scores, -1e30)
    fresh_max = jnp.maximum(running_max, jnp.max(scores, axis=2))
    shrink = jnp.exp(running_max - fresh_max)
    weights_raw = jnp.exp(scores - fresh_max[:, :, None])
    running_total = jnp.sum(weights_raw, axis=2)
    update = jnp.einsum(
        "hqk,khd->qhd",
        weights_raw.astype(jnp.bfloat16),
        value_heads,
        preferred_element_type=jnp.float32,
    )
    weighted = weighted * shrink.T[:, :, None] + update
    running_max, running_total, weighted = (fresh_max, running_total, weighted)
    mixed = (weighted / running_total.T[:, :, None]).reshape(row_count, H * DV)
    attended = (mixed * lax.rsqrt(jnp.mean(mixed * mixed, axis=1, keepdims=True) + 1e-05)).astype(
        jnp.bfloat16
    )
    hidden = (
        tokens.astype(jnp.float32)
        + jnp.dot(attended, out_weight, preferred_element_type=jnp.float32)
    ).astype(jnp.bfloat16)
    upsampled = (
        jnp.repeat(hidden, 2, axis=0).astype(jnp.float32) + skip[0].astype(jnp.float32)
    ).astype(jnp.bfloat16)
    padded = padded_2(upsampled, (("seq", 0),), 1)
    pre_act = (
        depth_weight[0] * padded[:-2]
        + depth_weight[1] * padded[1:-1]
        + depth_weight[2] * padded[2:]
    )
    act_value, pullback = jax.vjp(partial(jax.nn.gelu, approximate=True), pre_act)
    activated = act_value.astype(jnp.bfloat16)
    upstream = cotangent[0]
    grad_act = lax.dot_general(
        upstream, point_weight, (((1,), (1,)), ((), ())), preferred_element_type=jnp.float32
    )
    grad_pre = pullback(grad_act)[0].astype(jnp.bfloat16)
    fine_rows = grad_pre.shape[0]
    grad_wide = grad_pre.astype(jnp.float32)
    depth_term = jnp.stack(
        [
            jnp.sum(padded[offset : offset + fine_rows].astype(jnp.float32) * grad_wide, axis=0)
            for offset in range(3)
        ]
    )
    grad_padded = padded_2(grad_pre, (("seq", 0),), 1)
    grad_skip = (
        depth_weight[0] * grad_padded[2:]
        + depth_weight[1] * grad_padded[1:-1]
        + depth_weight[2] * grad_padded[:-2]
    ).astype(jnp.bfloat16)
    norm_scale = 1.0 / math.sqrt(lax.axis_size("dp") * lax.axis_size("seq") * fine_rows)
    point_term = lax.dot_general(
        activated, upstream, (((0,), (0,)), ((), ())), preferred_element_type=jnp.float32
    )
    point_total, depth_total = lax.psum((point_term, depth_term), ("dp", "seq"))
    grad_pointwise = (point_total * norm_scale).astype(jnp.bfloat16)
    return (grad_pointwise, depth_total * norm_scale, grad_skip[None])


def solution(mesh):
    return jax.shard_map(
        local,
        mesh=mesh,
        in_specs=(
            P("dp", "seq", None),
            P("dp", "seq", None),
            P("dp"),
            P(),
            P(),
            P(),
            P(),
            P(),
            P(),
            P("dp", "seq", None),
        ),
        out_specs=(P(), P(), P("dp", "seq", None)),
        check_vma=False,
    )
```

profile of v0, /device:TPU:1, one launch (start us, length us, event | category | flops | bytes accessed | tf_op | source)
XLA Modules:
  0.0 349.5 jit_solution(12524377417579679030)
XLA Ops:
  7.2 2.6 convolution_convert_fusion.1
  9.9 3.4 convolution_convert_fusion
  14.1 1.6 convolution_convert_fusion.2
  15.7 42.6 %all-gather.3.cloned.1.call-done = bf16[4096,256]{1,0:T(8,128)(2,1)} async-done(((bf16[256,256]{1,0:T(8,128)(2,1)}), bf16[4096,256]{1,0:T(8,128)(2,1)}) %all-gather.3.cloned.1.call-update) | async-done | bytes 2097168 | tf_op jit(solution)/shard_map/all_gather | solution.py:55
  58.2 4.1 %copy.15 = bf16[4096,256]{0,1:T(8,128)(2,1)} copy(bf16[4096,256]{1,0:T(8,128)(2,1)} %all-gather.3.cloned.1.call-done) | data formatting | bytes 4194304 | tf_op jit(solution)/shard_map/all_gather | solution.py:55
  62.3 4.1 %fusion = (f32[4,256]{1,0:T(4,128)S(1)}, f32[4,256,4096]{2,1,0:T(8,128)S(1)}) fusion(pred[4096]{0:T(1024)(128)(4,1)S(1)} %iota_compare_fusion, bf16[256,4,64]{0,2,1:T(8,128)(2,1)S(1)} %bitcast.49, bf16[4096,4,64]{0,2,1:T(8,128)(2,1)} %bitcast.47), kind=kOutput, calls=%fused_computation.2 | convolution fusion | flops 549452800 | bytes 19013632 | tf_op jit(solution)/shard_map/qhd,khd->hqk/dot_general | solution.py:61
  66.4 5.9 %copy-done.2 = f32[4,256,4096]{2,1,0:T(8,128)} copy-done((f32[4,256,4096]{2,1,0:T(8,128)}, f32[4,256,4096]{2,1,0:T(8,128)S(1)}, u32[]{:S(2)}) %copy-start.2) | copy-done | bytes 16777240
  72.4 4.0 %fusion.1 = f32[4,256]{1,0:T(4,128)S(1)} fusion(f32[4,256,4096]{2,1,0:T(8,128)S(1)} %get-tuple-element.17, f32[4,256]{1,0:T(4,128)S(1)} %get-tuple-element.15, pred[4096]{0:T(1024)(128)(4,1)S(1)} %iota_compare_fusion), kind=kLoop, calls=%fused_computation.3 | loop fusion | flops 16776192 | bytes 16789504 | tf_op jit(solution)/shard_map/reduce_sum | solution.py:69
  76.4 46.3 %all-gather.5.cloned.1.call-done = bf16[4096,768]{1,0:T(8,128)(2,1)} async-done(((bf16[256,768]{1,0:T(8,128)(2,1)}), bf16[4096,768]{1,0:T(8,128)(2,1)}) %all-gather.5.cloned.1.call-update) | async-done | bytes 6291472 | tf_op jit(solution)/shard_map/all_gather | solution.py:56
  122.7 8.6 %copy.16 = bf16[4096,768]{0,1:T(8,128)(2,1)} copy(bf16[4096,768]{1,0:T(8,128)(2,1)} %all-gather.5.cloned.1.call-done) | data formatting | bytes 12582912 | tf_op jit(solution)/shard_map/all_gather | solution.py:56
  131.3 10.3 %multiply_reduce_fusion = (f32[256]{0:T(256)S(1)}, f32[256,4,192]{0,2,1:T(8,128)S(1)}) fusion(f32[256,4]{0,1:T(4,128)S(1)} %bitcast.50, bf16[4096,4,192]{0,2,1:T(8,128)(2,1)} %bitcast.48, f32[4,256,4096]{2,1,0:T(8,128)} %copy-done.2, f32[4,256]{1,0:T(4,128)S(1)} %get-tuple-element.15, pred[4096]{0:T(1024)(128)(4,1)S(1)} %iota_compare_fusion, ...), kind=kOutput, calls=%fused_computation.68 | convolution fusion | flops 1628176128 | bytes 23872512 | tf_op jit(solution)/shard_map/hqk,khd->qhd/dot_general | solution.py:70
  142.5 2.7 broadcast_in_dim.33
  145.2 5.2 %convert_element_type.79 = f32[512,1536]{1,0:T(8,128)} reshape(f32[256,2,1536]{2,1,0:T(2,128)} %broadcast_in_dim.33) | data formatting | bytes 6291456 | tf_op jit(solution)/shard_map/convert_element_type | solution.py:87
  150.5 2.9 fusion.24
  153.4 3.1 collective-permute-start
  156.6 1.5 collective-permute-start.1
  158.1 2.8 collective-permute-done.1
  160.9 6.6 %fusion.27 = f32[1536,1536]{1,0:T(8,128)} fusion(bf16[512,1536]{1,0:T(8,128)(2,1)S(1)} %fusion.24, bf16[1,1536]{1,0:T(2,128)(2,1)S(1)} %collective-permute-done.1, bf16[1,1536]{1,0:T(2,128)(2,1)S(1)} %collective-permute-done, bf16[1,512,1536]{2,1,0:T(8,128)(2,1)S(1)} %copy-done.5, f32[1536]{0:T(1024)S(1)} %get-tuple-element.7, ...), kind=kOutput, calls=%fused_computation.41 | convolution fusion | flops 2434007040 | bytes 12607488 | tf_op jit(solution)/shard_map/dot_general | solution.py:117
  167.5 7.5 %fusion.17 = bf16[512,1536]{1,0:T(8,128)(2,1)S(1)} fusion(bf16[1,1536]{1,0:T(2,128)(2,1)S(1)} %collective-permute-done.1, bf16[512,1536]{1,0:T(8,128)(2,1)S(1)} %fusion.24, bf16[1,1536]{1,0:T(2,128)(2,1)S(1)} %collective-permute-done, bf16[1536,1536]{1,0:T(8,128)(2,1)} %param.18, bf16[1,512,1536]{2,1,0:T(8,128)(2,1)} %param.19, ...), kind=kOutput, calls=%fused_computation.28 | convolution fusion | flops 2442657792 | bytes 9461760 | tf_op jit(solution)/shard_map/dot_general | solution.py:98
  176.4 4.0 %collective-permute-start.3 = (bf16[1,1536]{1,0:T(2,128)(2,1)S(1)}, bf16[1,1536]{1,0:T(2,128)(2,1)S(1)}, u32[]{:S(2)}, u32[]{:S(2)}) collective-permute-start(bf16[1,1536]{1,0:T(2,128)(2,1)S(1)} %get-tuple-element.11), channel_id=1, source_target_pairs={{0,1},{1,2},{2,3},{3,4},{4,5},{5,6},{6,7},{7,8},{8,9},{9,10},{10,1... | collective-permute-start | bytes 9224 | tf_op jit(solution)/shard_map/ppermute | solution.py:21
  181.1 3.5 %fusion.18 = (f32[1536]{0:T(1024)S(1)}, f32[1536]{0:T(1024)S(1)}, f32[1536]{0:T(1024)S(1)}, bf16[1,512,1536]{2,1,0:T(8,128)(2,1)}) fusion(bf16[512,1536]{1,0:T(8,128)(2,1)S(1)} %fusion.17, bf16[512,1536]{1,0:T(8,128)(2,1)S(1)} %fusion.24, bf16[1,1536]{1,0:T(2,128)(2,1)S(1)} %collective-permute-done, bf16[1,1536]{1,0:T(2,128)(2,1)S(1)} %collective-permute-done.1, ...), kind=kLoop, calls=%fused_computation.29 | loop fusion | flops 23588352 | bytes 4767744 | tf_op jit(solution)/shard_map/reduce_sum | solution.py:106
  184.7 74.9 %psum.15 = f32[3,1536]{1,0:T(4,128)S(1)} all-reduce(f32[3,1536]{1,0:T(4,128)S(1)} %pad_maximum_fusion.5), channel_id=1, replica_groups=mesh['dp'=8,'seq'=16] {'dp','seq'}, use_global_device_ids=true, to_apply=%region_7.8 | all-reduce | flops 4608 | bytes 36864 | tf_op jit(solution)/shard_map/psum | solution.py:120
  260.2 75.5 %all-reduce.2.cloned.1.call-done = f32[1536,1536]{1,0:T(8,128)} async-done(((f32[1536,1536]{1,0:T(8,128)}), f32[1536,1536]{1,0:T(8,128)}) %all-reduce.2.cloned.1.call-update) | async-done | bytes 9437200 | tf_op jit(solution)/shard_map/psum | solution.py:120
  335.7 7.2 %multiply_convert_fusion = bf16[1536,1536]{1,0:T(8,128)(2,1)} fusion(f32[1536,1536]{1,0:T(8,128)} %all-reduce.2.cloned.1.call-done), kind=kLoop, calls=%fused_computation.5 | loop fusion | flops 4718592 | bytes 14155776 | tf_op jit(solution)/shard_map/convert_element_type | solution.py:121
  (34 shorter events, 3.9 us)
Async XLA Ops:
  7.2 134.5 %copy-start = (bf16[768,1536]{1,0:T(8,128)(2,1)S(1)}, bf16[768,1536]{1,0:T(8,128)(2,1)}, u32[]{:S(2)}) copy-start(bf16[768,1536]{1,0:T(8,128)(2,1)} %param.16) | copy-start | bytes 7077892
  7.2 6.9 %copy-start.3 = (bf16[1,256,1536]{2,1,0:T(8,128)(2,1)S(1)}, bf16[1,256,1536]{2,1,0:T(8,128)(2,1)}, u32[]{:S(2)}) copy-start(bf16[1,256,1536]{2,1,0:T(8,128)(2,1)} %param.10) | copy-start | bytes 2359300
  7.2 51.0 %all-gather.3.cloned.1.call-start = ((), (), s32[]{:S(2)}) async-start(), calls=%async_computation | async-start | bytes 2228224 | tf_op jit(solution)/shard_map/all_gather | solution.py:55
  9.8 112.8 %all-gather.5.cloned.1.call-start = ((), (), s32[]{:S(2)}) async-start(), calls=%async_computation.1 | async-start | bytes 6684672 | tf_op jit(solution)/shard_map/all_gather | solution.py:56
  13.4 322.4 %all-reduce.2.cloned.1.call-start = ((), (), s32[]{:S(2)}) async-start(), calls=%async_computation.2 | async-start | bytes 18874368 | tf_op jit(solution)/shard_map/psum | solution.py:120
  66.4 6.0 %copy-start.2 = (f32[4,256,4096]{2,1,0:T(8,128)}, f32[4,256,4096]{2,1,0:T(8,128)S(1)}, u32[]{:S(2)}) copy-start(f32[4,256,4096]{2,1,0:T(8,128)S(1)} %get-tuple-element.17) | copy-start | bytes 50331652
  150.5 7.6 %copy-start.4 = (f32[3,1536]{1,0:T(4,128)S(1)}, f32[3,1536]{1,0:T(4,128)}, u32[]{:S(2)}) copy-start(f32[3,1536]{1,0:T(4,128)} %param.17) | copy-start | bytes 55300
  150.5 10.4 %copy-start.5 = (bf16[1,512,1536]{2,1,0:T(8,128)(2,1)S(1)}, bf16[1,512,1536]{2,1,0:T(8,128)(2,1)}, u32[]{:S(2)}) copy-start(bf16[1,512,1536]{2,1,0:T(8,128)(2,1)} %param.19) | copy-start | bytes 4718596
  153.4 4.7 %collective-permute-start = (bf16[1,1536]{1,0:T(2,128)(2,1)S(1)}, bf16[1,1536]{1,0:T(2,128)(2,1)S(1)}, u32[]{:S(2)}, u32[]{:S(2)}) collective-permute-start(bf16[1,1536]{1,0:T(2,128)(2,1)S(1)} %get-tuple-element.12), channel_id=1, source_target_pairs={{0,1},{1,2},{2,3},{3,4},{4,5},{5,6},{6,7},{7,8},{8,9},{9,10},{10,1... | collective-permute-start | bytes 9224 | tf_op jit(solution)/shard_map/ppermute | solution.py:21
  156.6 4.4 %collective-permute-start.1 = (bf16[1,1536]{1,0:T(2,128)(2,1)S(1)}, bf16[1,1536]{1,0:T(2,128)(2,1)S(1)}, u32[]{:S(2)}, u32[]{:S(2)}) collective-permute-start(bf16[1,1536]{1,0:T(2,128)(2,1)S(1)} %get-tuple-element.13), channel_id=1, source_target_pairs={{1,0},{2,1},{3,2},{4,3},{5,4},{6,5},{7,6},{8,7},{9,8},{10,9},{11,1... | collective-permute-start | bytes 9224 | tf_op jit(solution)/shard_map/ppermute | solution.py:23
  175.1 5.3 %collective-permute-start.2 = (bf16[1,1536]{1,0:T(2,128)(2,1)S(1)}, bf16[1,1536]{1,0:T(2,128)(2,1)S(1)}, u32[]{:S(2)}, u32[]{:S(2)}) collective-permute-start(bf16[1,1536]{1,0:T(2,128)(2,1)S(1)} %get-tuple-element.10), channel_id=1, source_target_pairs={{1,0},{2,1},{3,2},{4,3},{5,4},{6,5},{7,6},{8,7},{9,8},{10,9},{11,1... | collective-permute-start | bytes 9224 | tf_op jit(solution)/shard_map/ppermute | solution.py:23
  176.4 4.8 %collective-permute-start.3 = (bf16[1,1536]{1,0:T(2,128)(2,1)S(1)}, bf16[1,1536]{1,0:T(2,128)(2,1)S(1)}, u32[]{:S(2)}, u32[]{:S(2)}) collective-permute-start(bf16[1,1536]{1,0:T(2,128)(2,1)S(1)} %get-tuple-element.11), channel_id=1, source_target_pairs={{0,1},{1,2},{2,3},{3,4},{4,5},{5,6},{6,7},{7,8},{8,9},{9,10},{10,1... | collective-permute-start | bytes 9224 | tf_op jit(solution)/shard_map/ppermute | solution.py:21
  335.7 7.2 %copy-start.1 = (bf16[768,1536]{1,0:T(8,128)(2,1)S(1)}, bf16[768,1536]{1,0:T(8,128)(2,1)}, u32[]{:S(2)}) copy-start(bf16[768,1536]{1,0:T(8,128)(2,1)} %param.16) | copy-start | bytes 7077892
Sparse Core Ops, SparseCore 0:
  10.7 47.4 all-gather.2
  60.9 61.6 all-gather.4
  167.6 168.0 all-reduce.1
where the time goes:
time: 350 us
  waiting for transfers between devices  168 us (48%)
  blocking collectives  74.9 us (21%)
  matrix products  36.9 us (11%)
  local copies, waits for them, and re-layouts  26.7 us (8%)
  other arithmetic  18.4 us (5%)
  between operations  14.6 us (4%)
  starting transfers between devices  9.98 us (3%)
    psum x1, waiting for transfers between devices, local(): point_total, depth_total = lax.psum((point_term, depth_term), ('dp', 'seq'))  75.5 us
    psum x1, blocking collectives, local(): point_total, depth_total = lax.psum((point_term, depth_term), ('dp', 'seq'))  74.9 us
    all_gather x1, waiting for transfers between devices, local(): value_piece = lax.all_gather(values, 'seq', axis=0, tiled=True)  46.3 us
    all_gather x1, waiting for transfers between devices, local(): key_piece = lax.all_gather(keys, 'seq', axis=0, tiled=True)  42.6 us
    dot_general x1, matrix products, local(): jnp.einsum('hqk,khd->qhd', weights_raw.astype(jnp.bfloat16), value_heads,...  10.3 us
    all_gather x1, local copies, waits for them, and re-layouts, local(): value_piece = lax.all_gather(values, 'seq', axis=0, tiled=True)  8.63 us
    dot_general x1, matrix products, local(): lax.dot_general(upstream, point_weight, (((1,), (1,)), ((), ())), preferr...  7.54 us
    convert_element_type x1, other arithmetic, local(): grad_pointwise = (point_total * norm_scale).astype(jnp.bfloat16)  7.24 us
  transfers between devices with their start and end apart: 7, of which 5 were waited for; matrix products, arithmetic and copies ran while one was open for 8% of the time, Pallas kernels for 0%

commit v1 on v0

--- a/solution.py
+++ b/solution.py
@@ -53,7 +53,9 @@
     running_max = jnp.full((H, row_count), -1e30, jnp.float32)
     weighted = jnp.zeros((row_count, H, DV), jnp.float32)
     key_piece = lax.all_gather(keys, "seq", axis=0, tiled=True)
-    value_piece = lax.all_gather(values, "seq", axis=0, tiled=True)
+    value_piece = jnp.concatenate(
+        lax.all_to_all(jnp.stack([values] * lax.axis_size("seq")), "seq", 0, 0), axis=0
+    )
     width = key_piece.shape[0]
     key_heads = key_piece.reshape(width, H, DH)
     value_heads = value_piece.reshape(width, H, DV)

time: 350 us -> 381 us (1.089)
  local copies, waits for them, and re-layouts: 26.7 us -> 40.8 us
  waiting for transfers between devices: 168 us -> 177 us
  starting transfers between devices: 9.98 us -> 17.3 us
    all_gather x1, waiting for transfers between devices: 42.6 us -> 97.4 us  [local(): key_piece = lax.all_gather(keys, 'seq', axis=0, tiled=True)]
    all_gather x1 -> x0, waiting for transfers between devices: 46.3 us -> none  [local(): value_piece = lax.all_gather(values, 'seq', axis=0, tiled=True)]
    another operation x0 -> x2, local copies, waits for them, and re-layouts: none -> 13.7 us  [the longest x1 10.4 us: local(): value_heads = value_piece.reshape(width, H, DV)]
    all_to_all x0 -> x1, local copies, waits for them, and re-layouts: none -> 9 us  [local(): lax.all_to_all(jnp.stack([values] * lax.axis_size('seq')), 'seq', 0, 0)]
    all_to_all x0 -> x1, starting transfers between devices: none -> 8.77 us  [local(): lax.all_to_all(jnp.stack([values] * lax.axis_size('seq')), 'seq', 0, 0)]
    all_gather x1 -> x0, local copies, waits for them, and re-layouts: 8.63 us -> none  [local(): value_piece = lax.all_gather(values, 'seq', axis=0, tiled=True)]
  transfers between devices with their start and end apart: 7 -> 7, of which waited for: 5 -> 4; matrix products, arithmetic and copies ran while one was open for 8% -> 8% of each run, Pallas kernels for 0% -> 0%
where the time goes in v1:
time: 381 us
  waiting for transfers between devices  177 us (46%)
  blocking collectives  76.3 us (20%)
  local copies, waits for them, and re-layouts  40.8 us (11%)
  matrix products  36.3 us (10%)
  other arithmetic  18.4 us (5%)
  starting transfers between devices  17.3 us (5%)
  between operations  14.9 us (4%)
    all_gather x1, waiting for transfers between devices, local(): key_piece = lax.all_gather(keys, 'seq', axis=0, tiled=True)  97.4 us
    psum x1, blocking collectives, local(): point_total, depth_total = lax.psum((point_term, depth_term), ('dp', 'seq'))  76.3 us
    psum x1, waiting for transfers between devices, local(): point_total, depth_total = lax.psum((point_term, depth_term), ('dp', 'seq'))  75.4 us
    dot_general x1, matrix products, local(): jnp.einsum('hqk,khd->qhd', weights_raw.astype(jnp.bfloat16), value_heads,...  10.5 us
    another operation x1, local copies, waits for them, and re-layouts, local(): value_heads = value_piece.reshape(width, H, DV)  10.4 us
    all_to_all x1, local copies, waits for them, and re-layouts, local(): lax.all_to_all(jnp.stack([values] * lax.axis_size('seq')), 'seq', 0, 0)  9 us
    all_to_all x1, starting transfers between devices, local(): lax.all_to_all(jnp.stack([values] * lax.axis_size('seq')), 'seq', 0, 0)  8.77 us
  transfers between devices with their start and end apart: 7, of which 4 were waited for; matrix products, arithmetic and copies ran while one was open for 8% of the time, Pallas kernels for 0%

profile of v1, /device:TPU:1, one launch (start us, length us, event | category | flops | bytes accessed | tf_op | source)
XLA Modules:
  0.0 380.6 jit_solution(8857652992178612775)
XLA Ops:
  7.2 2.5 convolution_convert_fusion.1
  9.8 2.7 convolution_convert_fusion
  12.7 3.3 stack.10
  15.9 8.8 %all-to-all-start = ((bf16[16,256,768]{1,2,0:T(8,128)(2,1)}), bf16[16,256,768]{1,2,0:T(8,128)(2,1)}, u32[]{:S(2)}, u32[]{:S(2)}) async-start(bf16[16,256,768]{1,2,0:T(8,128)(2,1)} %stack.10), calls=%async_computation | async-start | bytes 12582912 | tf_op jit(solution)/shard_map/all_to_all | solution.py:57
  27.0 97.4 %all-gather.2.cloned.1.call-done = bf16[4096,256]{1,0:T(8,128)(2,1)} async-done(((bf16[256,256]{1,0:T(8,128)(2,1)}), bf16[4096,256]{1,0:T(8,128)(2,1)}) %all-gather.2.cloned.1.call-update) | async-done | bytes 2097168 | tf_op jit(solution)/shard_map/all_gather | solution.py:55
  124.5 4.1 %copy.17 = bf16[4096,256]{0,1:T(8,128)(2,1)} copy(bf16[4096,256]{1,0:T(8,128)(2,1)} %all-gather.2.cloned.1.call-done) | data formatting | bytes 4194304 | tf_op jit(solution)/shard_map/all_gather | solution.py:55
  128.5 4.1 %fusion = (f32[4,256]{1,0:T(4,128)S(1)}, f32[4,256,4096]{2,1,0:T(8,128)S(1)}) fusion(pred[4096]{0:T(1024)(128)(4,1)S(1)} %iota_compare_fusion, bf16[256,4,64]{0,2,1:T(8,128)(2,1)S(1)} %bitcast.49, bf16[4096,4,64]{0,2,1:T(8,128)(2,1)} %bitcast.48), kind=kOutput, calls=%fused_computation.2 | convolution fusion | flops 549452800 | bytes 19013632 | tf_op jit(solution)/shard_map/qhd,khd->hqk/dot_general | solution.py:63
  132.7 5.7 %copy-done.2 = f32[4,256,4096]{2,1,0:T(8,128)} copy-done((f32[4,256,4096]{2,1,0:T(8,128)}, f32[4,256,4096]{2,1,0:T(8,128)S(1)}, u32[]{:S(2)}) %copy-start.2) | copy-done | bytes 16777240
  138.4 4.0 %fusion.1 = f32[4,256]{1,0:T(4,128)S(1)} fusion(f32[4,256,4096]{2,1,0:T(8,128)S(1)} %get-tuple-element.17, f32[4,256]{1,0:T(4,128)S(1)} %get-tuple-element.15, pred[4096]{0:T(1024)(128)(4,1)S(1)} %iota_compare_fusion), kind=kLoop, calls=%fused_computation.3 | loop fusion | flops 16776192 | bytes 16789504 | tf_op jit(solution)/shard_map/reduce_sum | solution.py:71
  142.4 9.0 %copy.19 = bf16[16,256,768]{1,0,2:T(8,128)(2,1)} copy(bf16[16,256,768]{1,2,0:T(8,128)(2,1)} %all-to-all-done) | data formatting | bytes 12582912 | tf_op jit(solution)/shard_map/all_to_all | solution.py:57
  151.4 10.4 %reshape_reshape.3 = bf16[4096,4,192]{0,2,1:T(8,128)(2,1)} reshape(bf16[16,256,768]{1,0,2:T(8,128)(2,1)} %copy.19) | data formatting | bytes 12582912 | tf_op jit(solution)/shard_map/reshape;reshape | solution.py:61
  161.8 10.5 %multiply_reduce_fusion = (f32[256]{0:T(256)S(1)}, f32[256,4,192]{0,2,1:T(8,128)S(1)}) fusion(f32[256,4]{0,1:T(4,128)S(1)} %bitcast.50, bf16[4096,4,192]{0,2,1:T(8,128)(2,1)} %reshape_reshape.3, f32[4,256,4096]{2,1,0:T(8,128)} %copy-done.2, f32[4,256]{1,0:T(4,128)S(1)} %get-tuple-element.15, pred[4096]{0:T(1024)(128)(4,1)S(1)} %iota_compare_fusion, ...), kind=kOutput, calls=%fused_computation.68 | convolution fusion | flops 1628176128 | bytes 23872512 | tf_op jit(solution)/shard_map/hqk,khd->qhd/dot_general | solution.py:72
  173.2 2.7 broadcast_in_dim.33
  175.9 5.2 %convert_element_type.79 = f32[512,1536]{1,0:T(8,128)} reshape(f32[256,2,1536]{2,1,0:T(2,128)} %broadcast_in_dim.33) | data formatting | bytes 6291456 | tf_op jit(solution)/shard_map/convert_element_type | solution.py:89
  181.2 2.9 fusion.24
  184.1 1.9 collective-permute-start
  187.4 3.0 collective-permute-done.1
  190.4 6.6 %fusion.27 = f32[1536,1536]{1,0:T(8,128)} fusion(bf16[512,1536]{1,0:T(8,128)(2,1)S(1)} %fusion.24, bf16[1,1536]{1,0:T(2,128)(2,1)S(1)} %collective-permute-done.1, bf16[1,1536]{1,0:T(2,128)(2,1)S(1)} %collective-permute-done, bf16[1,512,1536]{2,1,0:T(8,128)(2,1)S(1)} %copy-done.5, f32[1536]{0:T(1024)S(1)} %get-tuple-element.7, ...), kind=kOutput, calls=%fused_computation.41 | convolution fusion | flops 2434007040 | bytes 12607488 | tf_op jit(solution)/shard_map/dot_general | solution.py:119
  197.0 7.5 %fusion.17 = bf16[512,1536]{1,0:T(8,128)(2,1)S(1)} fusion(bf16[1,1536]{1,0:T(2,128)(2,1)S(1)} %collective-permute-done.1, bf16[512,1536]{1,0:T(8,128)(2,1)S(1)} %fusion.24, bf16[1,1536]{1,0:T(2,128)(2,1)S(1)} %collective-permute-done, bf16[1536,1536]{1,0:T(8,128)(2,1)} %param.18, bf16[1,512,1536]{2,1,0:T(8,128)(2,1)} %param.19, ...), kind=kOutput, calls=%fused_computation.28 | convolution fusion | flops 2442657792 | bytes 9461760 | tf_op jit(solution)/shard_map/dot_general | solution.py:100
  205.9 4.0 %collective-permute-start.3 = (bf16[1,1536]{1,0:T(2,128)(2,1)S(1)}, bf16[1,1536]{1,0:T(2,128)(2,1)S(1)}, u32[]{:S(2)}, u32[]{:S(2)}) collective-permute-start(bf16[1,1536]{1,0:T(2,128)(2,1)S(1)} %get-tuple-element.11), channel_id=1, source_target_pairs={{0,1},{1,2},{2,3},{3,4},{4,5},{5,6},{6,7},{7,8},{8,9},{9,10},{10,1... | collective-permute-start | bytes 9224 | tf_op jit(solution)/shard_map/ppermute | solution.py:21
  210.6 3.5 fusion.18
  214.2 76.3 %psum.15 = f32[3,1536]{1,0:T(4,128)S(1)} all-reduce(f32[3,1536]{1,0:T(4,128)S(1)} %pad_maximum_fusion.5), channel_id=1, replica_groups=mesh['dp'=8,'seq'=16] {'dp','seq'}, use_global_device_ids=true, to_apply=%region_7.8 | all-reduce | flops 4608 | bytes 36864 | tf_op jit(solution)/shard_map/psum | solution.py:122
  291.1 75.4 %all-reduce.2.cloned.1.call-done = f32[1536,1536]{1,0:T(8,128)} async-done(((f32[1536,1536]{1,0:T(8,128)}), f32[1536,1536]{1,0:T(8,128)}) %all-reduce.2.cloned.1.call-update) | async-done | bytes 9437200 | tf_op jit(solution)/shard_map/psum | solution.py:122
  366.5 7.2 %multiply_convert_fusion = bf16[1536,1536]{1,0:T(8,128)(2,1)} fusion(f32[1536,1536]{1,0:T(8,128)} %all-reduce.2.cloned.1.call-done), kind=kLoop, calls=%fused_computation.5 | loop fusion | flops 4718592 | bytes 14155776 | tf_op jit(solution)/shard_map/convert_element_type | solution.py:123
  (36 shorter events, 6.8 us)
Async XLA Ops:
  7.2 165.2 %copy-start = (bf16[768,1536]{1,0:T(8,128)(2,1)S(1)}, bf16[768,1536]{1,0:T(8,128)(2,1)}, u32[]{:S(2)}) copy-start(bf16[768,1536]{1,0:T(8,128)(2,1)} %param.16) | copy-start | bytes 7077892
  7.2 117.3 %all-gather.2.cloned.1.call-start = ((), (), s32[]{:S(2)}) async-start(), calls=%async_computation.1 | async-start | bytes 2228224 | tf_op jit(solution)/shard_map/all_gather | solution.py:55
  15.9 9.5 %copy-start.3 = (bf16[1,256,1536]{2,1,0:T(8,128)(2,1)S(1)}, bf16[1,256,1536]{2,1,0:T(8,128)(2,1)}, u32[]{:S(2)}) copy-start(bf16[1,256,1536]{2,1,0:T(8,128)(2,1)} %param.10) | copy-start | bytes 2359300
  15.9 126.4 %all-to-all-start = ((bf16[16,256,768]{1,2,0:T(8,128)(2,1)}), bf16[16,256,768]{1,2,0:T(8,128)(2,1)}, u32[]{:S(2)}, u32[]{:S(2)}) async-start(bf16[16,256,768]{1,2,0:T(8,128)(2,1)} %stack.10), calls=%async_computation | async-start | bytes 12582912 | tf_op jit(solution)/shard_map/all_to_all | solution.py:57
  24.7 341.8 %all-reduce.2.cloned.1.call-start = ((), (), s32[]{:S(2)}) async-start(), calls=%async_computation.2 | async-start | bytes 18874368 | tf_op jit(solution)/shard_map/psum | solution.py:122
  132.6 5.7 %copy-start.2 = (f32[4,256,4096]{2,1,0:T(8,128)}, f32[4,256,4096]{2,1,0:T(8,128)S(1)}, u32[]{:S(2)}) copy-start(f32[4,256,4096]{2,1,0:T(8,128)S(1)} %get-tuple-element.17) | copy-start | bytes 50331652
  181.2 6.2 %copy-start.4 = (f32[3,1536]{1,0:T(4,128)S(1)}, f32[3,1536]{1,0:T(4,128)}, u32[]{:S(2)}) copy-start(f32[3,1536]{1,0:T(4,128)} %param.17) | copy-start | bytes 55300
  181.2 9.3 %copy-start.5 = (bf16[1,512,1536]{2,1,0:T(8,128)(2,1)S(1)}, bf16[1,512,1536]{2,1,0:T(8,128)(2,1)}, u32[]{:S(2)}) copy-start(bf16[1,512,1536]{2,1,0:T(8,128)(2,1)} %param.19) | copy-start | bytes 4718596
  184.1 3.3 collective-permute-start
  186.1 4.4 %collective-permute-start.1 = (bf16[1,1536]{1,0:T(2,128)(2,1)S(1)}, bf16[1,1536]{1,0:T(2,128)(2,1)S(1)}, u32[]{:S(2)}, u32[]{:S(2)}) collective-permute-start(bf16[1,1536]{1,0:T(2,128)(2,1)S(1)} %get-tuple-element.13), channel_id=1, source_target_pairs={{1,0},{2,1},{3,2},{4,3},{5,4},{6,5},{7,6},{8,7},{9,8},{10,9},{11,1... | collective-permute-start | bytes 9224 | tf_op jit(solution)/shard_map/ppermute | solution.py:23
  204.6 5.3 %collective-permute-start.2 = (bf16[1,1536]{1,0:T(2,128)(2,1)S(1)}, bf16[1,1536]{1,0:T(2,128)(2,1)S(1)}, u32[]{:S(2)}, u32[]{:S(2)}) collective-permute-start(bf16[1,1536]{1,0:T(2,128)(2,1)S(1)} %get-tuple-element.10), channel_id=1, source_target_pairs={{1,0},{2,1},{3,2},{4,3},{5,4},{6,5},{7,6},{8,7},{9,8},{10,9},{11,1... | collective-permute-start | bytes 9224 | tf_op jit(solution)/shard_map/ppermute | solution.py:23
  205.9 4.8 %collective-permute-start.3 = (bf16[1,1536]{1,0:T(2,128)(2,1)S(1)}, bf16[1,1536]{1,0:T(2,128)(2,1)S(1)}, u32[]{:S(2)}, u32[]{:S(2)}) collective-permute-start(bf16[1,1536]{1,0:T(2,128)(2,1)S(1)} %get-tuple-element.11), channel_id=1, source_target_pairs={{0,1},{1,2},{2,3},{3,4},{4,5},{5,6},{6,7},{7,8},{8,9},{9,10},{10,1... | collective-permute-start | bytes 9224 | tf_op jit(solution)/shard_map/ppermute | solution.py:21
  366.5 7.2 %copy-start.1 = (bf16[768,1536]{1,0:T(8,128)(2,1)S(1)}, bf16[768,1536]{1,0:T(8,128)(2,1)}, u32[]{:S(2)}) copy-start(bf16[768,1536]{1,0:T(8,128)(2,1)} %param.16) | copy-start | bytes 7077892
Sparse Core Ops, SparseCore 0:
  10.7 113.6 all-gather.1
  197.1 169.3 all-reduce.1
